TPU v7x, 256 devices: a whole 4x4x8 slice. The times are simulated.
256 devices in a mesh: dp: 8 (over y, x_hi), seq: 16 (over z, core), cell: 2 (over x_lo).
Axes of the slice: x: 4 (x_hi: 2, x_lo: 2; x = x_hi * 2 + x_lo), y: 4, z: 8, core: 2. Of those that a mesh axis runs over, the one named last changes fastest.
Arguments:
- cells: bfloat16 [8, 16384, 768], P('dp', ('seq', 'cell')), may hold values from -64 to 64
- anchor_ids: int32 [8, 16384], P('dp', ('seq', 'cell')), may hold values from 0 to 511, as said below
- cell_counts: int32 [8, 32], P('dp', ('seq', 'cell')), may hold values from 384 to 512, as said below
- anchor_gain: float32 [768], replicated, may hold values from 0.5 to 1.5
- w_query: bfloat16 [768, 768], replicated, may hold values from -0.21875 to 0.21875
- w_keyval: bfloat16 [768, 1536], replicated, may hold values from -0.21875 to 0.21875
- w_out: bfloat16 [768, 768], replicated, may hold values from -0.21875 to 0.21875
- cotangent: bfloat16 [8, 16384, 768], P('dp', ('seq', 'cell')), may hold values from -6 to 6
Outputs:
- cell_update: bfloat16 [8, 16384, 768], P('dp', ('seq', 'cell'))
- grad_query: float32 [768, 768], P(('seq', 'cell'))
- grad_keyval: float32 [768, 1536], P(('seq', 'cell'))
- grad_out: float32 [768, 768], P(('seq', 'cell'))
Inputs may be any that keep to these rules, and one draw needn't show every extreme that they name: `anchor_ids`: anchors o * 16 to (o + 1) * 16 - 1 belong to owner o of the sample. The valid cells of one device name anchors of any one owner at most 32 times, and each device's first 32 cells all name anchors of its own index. `cell_counts`: in every sample some device has all 512 cells valid.
All inputs are finite; a program needn't handle non-finite values.
Results may differ from a plain program's by a relative error of at most 0.035.
The roundings to bfloat16 on the way count: a program that leaves them out, or rounds other values in their place, can miss the bound.
Values may be sent and summed in bfloat16 or wider, within the bound.
A program may use at most 128 MiB of HBM per device.

v0:
```python
import math

import jax
import jax.numpy as jnp
from jax import lax
from jax.sharding import PartitionSpec as P

HEADS = 12
HEAD = 64
A_DEV = 16


def split_heads(matrix):
    return matrix.reshape(matrix.shape[0], HEADS, matrix.shape[1] // HEADS)


def paired_product(left_low, right_full):
    upper_part = right_full.astype(jnp.bfloat16)
    lower_part = (right_full - upper_part.astype(jnp.float32)).astype(jnp.bfloat16)
    first = jnp.einsum("ad,ae->de", left_low, upper_part, preferred_element_type=jnp.float32)
    second = jnp.einsum("ad,ae->de", left_low, lower_part, preferred_element_type=jnp.float32)
    return first + second


def shards(cells, anchor_ids, cell_counts, anchor_gain, w_query, w_keyval, w_out, cotangent):
    cell_rows = cells[0]
    cell_ids = anchor_ids[0]
    row_limit = cell_counts[0, 0]
    n_rows, model_width = cell_rows.shape
    owners = lax.axis_size(("seq", "cell"))
    capacity = 2 * n_rows // owners
    score_scale = 1.0 / math.sqrt(HEAD)
    valid_mask = jnp.arange(n_rows, dtype=jnp.int32) < row_limit
    is_valid = valid_mask.astype(jnp.float32)
    owner_of = cell_ids // A_DEV
    local_id = cell_ids - owner_of * A_DEV
    owner_hot = (
        (owner_of[:, None] == jnp.arange(owners, dtype=jnp.int32)[None, :]) & valid_mask[:, None]
    ).astype(jnp.int32)
    slot_rank = jnp.sum((jnp.cumsum(owner_hot, axis=0) - 1) * owner_hot, axis=1)
    slot_index = jnp.where(valid_mask, owner_of * capacity + slot_rank, -1)
    dispatch = slot_index[None, :] == jnp.arange(owners * capacity, dtype=jnp.int32)[:, None]
    send_rows = jnp.dot(
        dispatch.astype(jnp.bfloat16), cell_rows, preferred_element_type=jnp.float32
    ).astype(jnp.bfloat16)
    send_ids = jnp.sum(jnp.where(dispatch, local_id[None, :] + 1, 0), axis=1)
    got_rows, got_ids = (
        lax.all_to_all(
            send_rows.reshape(owners, capacity, model_width),
            ("seq", "cell"),
            split_axis=0,
            concat_axis=0,
            tiled=True,
        ),
        lax.all_to_all(
            send_ids.reshape(owners, capacity),
            ("seq", "cell"),
            split_axis=0,
            concat_axis=0,
            tiled=True,
        ),
    )
    got_rows = got_rows.reshape(owners * capacity, model_width)
    pool_hot = (
        got_ids.reshape(1, owners * capacity) == jnp.arange(1, A_DEV + 1, dtype=jnp.int32)[:, None]
    )
    pooled_sum = jnp.dot(
        pool_hot.astype(jnp.bfloat16), got_rows, preferred_element_type=jnp.float32
    )
    anchor_count = jnp.sum(pool_hot.astype(jnp.float32), axis=1)
    pooled = pooled_sum / jnp.maximum(anchor_count, 1.0)[:, None]
    normed = (
        pooled * lax.rsqrt(jnp.mean(pooled * pooled, axis=1) + 1e-06)[:, None] * anchor_gain
    ).astype(jnp.bfloat16)
    keyval = jnp.dot(normed, w_keyval, preferred_element_type=jnp.float32).astype(jnp.bfloat16)
    pair_block = lax.all_gather(keyval, "cell", axis=0, tiled=True)
    queries = jnp.dot(cell_rows, w_query, preferred_element_type=jnp.float32).astype(jnp.bfloat16)
    query_heads = split_heads(queries)

    def logits_for(key_piece):
        key_heads = split_heads(key_piece[:, :model_width])
        return (
            jnp.einsum("chd,ahd->hca", query_heads, key_heads, preferred_element_type=jnp.float32)
            * score_scale
        )

    key_piece = lax.all_gather(pair_block, "seq", axis=0, tiled=True)
    forward_row_peak = jnp.full((HEADS, n_rows), -jnp.inf, jnp.float32)
    forward_row_total = jnp.zeros((HEADS, n_rows), jnp.float32)
    weighted = jnp.zeros((HEADS, n_rows, HEAD), jnp.float32)
    logits = logits_for(key_piece)
    new_peak = jnp.max(logits, axis=2)
    factor = jnp.exp(forward_row_peak - new_peak)
    exp_terms = jnp.exp(logits - new_peak[:, :, None])
    value_heads = split_heads(key_piece[:, model_width:])
    weighted = weighted * factor[:, :, None] + jnp.einsum(
        "hca,ahd->hcd",
        exp_terms.astype(jnp.bfloat16),
        value_heads,
        preferred_element_type=jnp.float32,
    )
    forward_row_total = forward_row_total * factor + jnp.sum(exp_terms, axis=2)
    row_peak, row_total, weighted = (new_peak, forward_row_total, weighted)
    attended = (
        jnp.transpose(weighted / row_total[:, :, None], (1, 0, 2))
        .reshape(n_rows, model_width)
        .astype(jnp.bfloat16)
    )
    cell_delta = jnp.dot(attended, w_out, preferred_element_type=jnp.float32) * is_valid[:, None]
    cell_update = cell_delta.astype(jnp.bfloat16)[None]
    masked = cotangent[0] * valid_mask[:, None].astype(jnp.bfloat16)
    grad_out_part = jnp.einsum("cd,ce->de", attended, masked, preferred_element_type=jnp.float32)
    d_attended = jnp.einsum("ce,de->cd", masked, w_out, preferred_element_type=jnp.float32).astype(
        jnp.bfloat16
    )
    d_heads = split_heads(d_attended)
    row_delta = jnp.transpose(
        jnp.sum(d_heads.astype(jnp.float32) * split_heads(attended).astype(jnp.float32), axis=2)
    )
    key_piece = lax.all_gather(pair_block, "seq", axis=0, tiled=True)
    logits = logits_for(key_piece)
    key_heads = split_heads(key_piece[:, :model_width])
    value_heads = split_heads(key_piece[:, model_width:])
    attn_prob = jnp.exp(logits - row_peak[:, :, None]) / row_total[:, :, None]
    d_prob = jnp.einsum("chd,ahd->hca", d_heads, value_heads, preferred_element_type=jnp.float32)
    d_logits = (attn_prob * (d_prob - row_delta[:, :, None]) * score_scale).astype(jnp.bfloat16)
    d_query = jnp.einsum("hca,ahd->chd", d_logits, key_heads, preferred_element_type=jnp.float32)
    d_key = jnp.einsum("hca,chd->ahd", d_logits, query_heads, preferred_element_type=jnp.float32)
    d_value = jnp.einsum(
        "hca,chd->ahd", attn_prob.astype(jnp.bfloat16), d_heads, preferred_element_type=jnp.float32
    )
    piece_rows = key_piece.shape[0]
    term = jnp.concatenate(
        [d_key.reshape(piece_rows, model_width), d_value.reshape(piece_rows, model_width)], axis=1
    )
    key_terms = term
    d_query, key_terms = (d_query, key_terms)
    d_query = d_query.reshape(n_rows, model_width).astype(jnp.bfloat16)
    grad_query_part = jnp.einsum(
        "cd,ce->de", cell_rows, d_query, preferred_element_type=jnp.float32
    )
    owner_grads = lax.psum_scatter(
        key_terms.astype(jnp.bfloat16), ("seq", "cell"), scatter_dimension=0, tiled=True
    ).astype(jnp.float32)
    grad_keyval_part = paired_product(normed, owner_grads)
    shares = (
        lax.psum_scatter(
            grad_query_part.astype(jnp.bfloat16), ("seq", "cell"), scatter_dimension=0, tiled=True
        ).astype(jnp.float32),
        lax.psum_scatter(
            grad_keyval_part.astype(jnp.bfloat16), ("seq", "cell"), scatter_dimension=0, tiled=True
        ).astype(jnp.float32),
        lax.psum_scatter(
            grad_out_part.astype(jnp.bfloat16), ("seq", "cell"), scatter_dimension=0, tiled=True
        ).astype(jnp.float32),
    )
    grad_query, grad_keyval, grad_out = (
        lax.psum(shares[0].astype(jnp.bfloat16), "dp").astype(jnp.float32),
        lax.psum(shares[1].astype(jnp.bfloat16), "dp").astype(jnp.float32),
        lax.psum(shares[2].astype(jnp.bfloat16), "dp").astype(jnp.float32),
    )
    return (cell_update, grad_query, grad_keyval, grad_out)


def solution(mesh):
    return jax.shard_map(
        shards,
        mesh=mesh,
        in_specs=(
            P("dp", ("seq", "cell"), None),
            P("dp", ("seq", "cell")),
            P("dp", ("seq", "cell")),
            P(),
            P(),
            P(),
            P(),
            P("dp", ("seq", "cell"), None),
        ),
        out_specs=(
            P("dp", ("seq", "cell"), None),
            P(("seq", "cell"), None),
            P(("seq", "cell"), None),
            P(("seq", "cell"), None),
        ),
        check_vma=False,
    )
```

profile of v0, /device:TPU:32, one launch (start us, length us, event | category | flops | bytes accessed | tf_op | source)
XLA Modules:
  0.0 816.6 jit_solution(9952618093060738055)
XLA Ops:
  8.0 0.7 subtract_add_fusion
  8.7 0.7 add_select_fusion
  9.4 1.2 reduce-window.6
  10.6 0.2 slice_reduce_fusion
  10.8 0.7 add_select_fusion.1
  11.5 0.1 fusion.32
  11.7 0.3 select_reduce_fusion
  11.9 0.7 all_to_all.9
  12.6 9.7 %all-to-all-start = ((s32[32,1,32]{2,1,0:T(1,128)}), s32[32,1,32]{2,1,0:T(1,128)S(1)}, u32[]{:S(2)}, u32[]{:S(2)}) async-start(s32[32,1,32]{2,1,0:T(1,128)} %all_to_all.9), calls=%async_computation | async-start | bytes 32768 | tf_op jit(solution)/shard_map/all_to_all | solution.py:55
  22.3 3.3 fusion.11
  25.6 3.7 all-to-all-done
  29.3 5.8 all-to-all-start.1
  35.1 0.5 broadcast.221
  35.6 0.7 reduce.5
  36.3 0.1 eq.61
  36.4 0.2 fusion.30
  36.6 37.9 %all-to-all-done.1 = bf16[32,32,768]{2,1,0:T(8,128)(2,1)} async-done(((bf16[32,32,768]{2,1,0:T(8,128)(2,1)}), bf16[32,32,768]{2,1,0:T(8,128)(2,1)}, u32[]{:S(2)}, u32[]{:S(2)}) %all-to-all-start.1) | async-done | bytes 1572896 | tf_op jit(solution)/shard_map/all_to_all | solution.py:48
  74.5 1.9 multiply_reduce_fusion.2
  76.4 0.1 multiply_convert_fusion.2
  76.5 0.6 copy-done.7
  77.1 0.4 convolution_convert_fusion
  77.5 4.9 all_gather.7
  82.4 0.2 reduce-scatter.15.cloned.1.call-start
  82.6 2.3 convolution_convert_fusion.4
  84.9 1.2 copy.47
  86.1 2.3 convolution_convert_fusion.3
  88.5 1.2 copy.52
  89.6 29.5 %all-gather.2.cloned.1.call-done = bf16[512,1536]{1,0:T(8,128)(2,1)} async-done(((bf16[32,1536]{1,0:T(8,128)(2,1)}), bf16[512,1536]{1,0:T(8,128)(2,1)}) %all-gather.2.cloned.1.call-update) | async-done | bytes 1572880 | tf_op jit(solution)/shard_map/all_gather | solution.py:87
  119.1 2.6 fusion.48
  121.8 1.4 copy.49
  123.2 3.0 multiply_reduce_fusion
  126.2 2.1 fusion.1
  128.3 2.5 copy-done.2
  130.8 2.3 copy.50
  133.1 7.6 fusion.17
  140.7 0.8 copy-done.3
  141.5 0.1 copy-done.5
  141.6 0.2 copy-done.6
  141.8 3.4 multiply_reduce_fusion.1
  145.3 4.2 multiply_convert_fusion
  149.5 2.0 convolution_convert_fusion.5
  151.5 0.6 copy-done.1
  152.1 1.3 pad_maximum_fusion
  153.5 2.6 copy.65
  156.1 0.0 reduce-scatter.13.cloned.1.call-start
  156.1 4.0 convolution_convert_fusion.6
  160.1 0.8 fusion.16
  160.9 1.5 copy.63
  162.4 3.3 convolution_convert_fusion.1
  165.7 0.0 reduce-scatter.9.cloned.1.call-start
  165.8 103.1 %reduce-scatter.15.cloned.1.call-done = bf16[16,1536]{1,0:T(8,128)(2,1)} async-done(((bf16[512,1536]{1,0:T(8,128)(2,1)}), bf16[16,1536]{1,0:T(8,128)(2,1)}) %reduce-scatter.15.cloned.1.call-update) | async-done | bytes 49168
  268.9 1.0 copy.66
  269.9 1.6 fusion.49
  271.5 2.2 add_convert_fusion
  273.8 114.1 %reduce-scatter.13.cloned.1.call-done = bf16[24,768]{1,0:T(8,128)(2,1)} async-done(((bf16[768,768]{1,0:T(8,128)(2,1)}), bf16[24,768]{1,0:T(8,128)(2,1)}) %reduce-scatter.13.cloned.1.call-update) | async-done | bytes 36880
  387.9 1.6 copy.64
  389.5 117.0 %reduce-scatter.11.cloned.1.call-done = bf16[24,768]{1,0:T(8,128)(2,1)} async-done(((bf16[768,768]{1,0:T(8,128)(2,1)}), bf16[24,768]{1,0:T(8,128)(2,1)}) %reduce-scatter.11.cloned.1.call-update) | async-done | bytes 36880 | tf_op jit(solution)/shard_map/reduce_scatter | solution.py:153
  506.6 121.3 %reduce-scatter.9.cloned.1.call-done = bf16[24,1536]{1,0:T(8,128)(2,1)} async-done(((bf16[768,1536]{1,0:T(8,128)(2,1)}), bf16[24,1536]{1,0:T(8,128)(2,1)}) %reduce-scatter.9.cloned.1.call-update) | async-done | bytes 73744 | tf_op jit(solution)/shard_map/reduce_scatter | solution.py:150
  627.9 3.2 fusion.20
  631.1 91.8 %all-reduce.6.cloned.1.call-done = (bf16[24,768]{0,1:T(8,128)(2,1)}, bf16[24,768]{1,0:T(8,128)(2,1)}) async-done(((bf16[24,768]{0,1:T(8,128)(2,1)}, bf16[24,768]{1,0:T(8,128)(2,1)}), (bf16[24,768]{0,1:T(8,128)(2,1)}, bf16[24,768]{1,0:T(8,128)(2,1)})) %all-reduce.6.cloned.1.call-update) | async-done | bytes 73744 | tf_op jit(solution)/shard_map/psum | solution.py:158
  723.0 1.4 convert_element_type.139
  724.4 1.7 copy.57
  726.1 82.2 %all-reduce.4.cloned.1.call-done = bf16[24,1536]{1,0:T(8,128)(2,1)} async-done(((bf16[24,1536]{1,0:T(8,128)(2,1)}), bf16[24,1536]{1,0:T(8,128)(2,1)}) %all-reduce.4.cloned.1.call-update) | async-done | bytes 73744 | tf_op jit(solution)/shard_map/psum | solution.py:159
  808.2 1.6 convert_element_type.137
  (39 shorter events, 0.4 us)
Async XLA Ops:
  7.2 69.9 %copy-start = (bf16[768,1536]{1,0:T(8,128)(2,1)S(1)}, bf16[768,1536]{1,0:T(8,128)(2,1)}, u32[]{:S(2)}) copy-start(bf16[768,1536]{1,0:T(8,128)(2,1)} %param.13) | copy-start | bytes 7077892
  12.6 16.7 %all-to-all-start = ((s32[32,1,32]{2,1,0:T(1,128)}), s32[32,1,32]{2,1,0:T(1,128)S(1)}, u32[]{:S(2)}, u32[]{:S(2)}) async-start(s32[32,1,32]{2,1,0:T(1,128)} %all_to_all.9), calls=%async_computation | async-start | bytes 32768 | tf_op jit(solution)/shard_map/all_to_all | solution.py:55
  25.6 50.8 %copy-start.9 = (f32[768]{0:T(1024)S(1)}, f32[768]{0:T(1024)}, u32[]{:S(2)}) copy-start(f32[768]{0:T(1024)} %param.11) | copy-start | bytes 9220
  29.3 45.2 %all-to-all-start.1 = ((bf16[32,32,768]{2,1,0:T(8,128)(2,1)}), bf16[32,32,768]{2,1,0:T(8,128)(2,1)}, u32[]{:S(2)}, u32[]{:S(2)}) async-start(bf16[32,32,768]{2,1,0:T(8,128)(2,1)} %bitcast.101), calls=%async_computation.1 | async-start | bytes 3145728 | tf_op jit(solution)/shard_map/all_to_all | solution.py:48
  35.1 84.1 %all-gather.2.cloned.1.call-start = ((), (), s32[]{:S(2)}) async-start(), calls=%async_computation.6 | async-start | bytes 1671168 | tf_op jit(solution)/shard_map/all_gather | solution.py:87
  76.5 0.6 copy-start.7
  82.4 186.5 %reduce-scatter.15.cloned.1.call-start = ((), (), s32[]{:S(2)}) async-start(), calls=%async_computation.11 | async-start | bytes 1622016
  126.2 4.6 copy-start.2
  133.1 8.4 %copy-start.3 = (f32[12,512,512]{1,2,0:T(8,128)S(1)}, f32[12,512,512]{1,2,0:T(8,128)}, u32[]{:S(2)}) copy-start(f32[12,512,512]{1,2,0:T(8,128)} %copy-done.2) | copy-start | bytes 37748740
  133.1 8.5 %copy-start.5 = (bf16[512,768]{0,1:T(8,128)(2,1)S(1)}, bf16[512,768]{0,1:T(8,128)(2,1)}, u32[]{:S(2)}) copy-start(bf16[512,768]{0,1:T(8,128)(2,1)} %copy.52) | copy-start | bytes 2359300
  133.1 8.7 %copy-start.6 = (bf16[512,768]{0,1:T(8,128)(2,1)S(1)}, bf16[512,768]{0,1:T(8,128)(2,1)}, u32[]{:S(2)}) copy-start(bf16[512,768]{0,1:T(8,128)(2,1)} %copy.50) | copy-start | bytes 2359300
  145.2 4.2 copy-start.4
  149.5 2.7 copy-start.1
  156.1 231.9 %reduce-scatter.13.cloned.1.call-start = ((), (), s32[]{:S(2)}) async-start(), calls=%async_computation.10 | async-start | bytes 1216512
  156.1 4.0 copy-start.10
  162.4 107.5 %copy-start.8 = (bf16[16,768]{1,0:T(8,128)(2,1)S(1)}, bf16[16,768]{1,0:T(8,128)(2,1)}, u32[]{:S(2)}) copy-start(bf16[16,768]{1,0:T(8,128)(2,1)} %copy-done.7) | copy-start | bytes 73732
  162.4 344.1 %reduce-scatter.11.cloned.1.call-start = ((), (), s32[]{:S(2)}) async-start(), calls=%async_computation.9 | async-start | bytes 1216512 | tf_op jit(solution)/shard_map/reduce_scatter | solution.py:153
  165.7 462.2 %reduce-scatter.9.cloned.1.call-start = ((), (), s32[]{:S(2)}) async-start(), calls=%async_computation.7 | async-start | bytes 2433024 | tf_op jit(solution)/shard_map/reduce_scatter | solution.py:150
  273.8 449.2 %all-reduce.6.cloned.1.call-start = ((), (), s32[]{:S(2)}) async-start(), calls=%async_computation.12 | async-start | bytes 466944 | tf_op jit(solution)/shard_map/psum | solution.py:158
  506.5 301.7 %all-reduce.4.cloned.1.call-start = ((), (), s32[]{:S(2)}) async-start(), calls=%async_computation.8 | async-start | bytes 147456 | tf_op jit(solution)/shard_map/psum | solution.py:159
Sparse Core Ops, SparseCore 0:
  82.5 36.5 all-gather.1
  156.2 112.6 reduce-scatter.14
  271.5 116.3 reduce-scatter.12
  390.3 116.1 reduce-scatter.10
  509.1 118.7 reduce-scatter.8
  630.7 92.2 all-reduce.5
  725.6 82.5 all-reduce.3
where the time goes:
time: 818 us; the launch traced here: 817 us
  waiting for transfers between devices  701 us (86%)
  matrix products  45.5 us (6%)
  local copies, waits for them, and re-layouts  23.4 us (3%)
  starting transfers between devices  15.9 us (2%)
  between operations  15.1 us (2%)
  other arithmetic  11.1 us (1%)
    unnamed x9, waiting for transfers between devices  217 us
    reduce_scatter x1, waiting for transfers between devices, shards(): lax.psum_scatter(grad_keyval_part.astype(jnp.bfloat16), ('seq', 'cell'),...  121 us
    reduce_scatter x1, waiting for transfers between devices, shards(): lax.psum_scatter(grad_out_part.astype(jnp.bfloat16), ('seq', 'cell'), sca...  117 us
    psum x1, waiting for transfers between devices, shards(): lax.psum(shares[0].astype(jnp.bfloat16), 'dp').astype(jnp.float32)  91.8 us
    psum x1, waiting for transfers between devices, shards(): lax.psum(shares[1].astype(jnp.bfloat16), 'dp').astype(jnp.float32)  82.2 us
    all_to_all x1, waiting for transfers between devices, shards(): lax.all_to_all(send_rows.reshape(owners, capacity, model_width), ('seq',...  37.9 us
    all_gather x1, waiting for transfers between devices, shards(): key_piece = lax.all_gather(pair_block, 'seq', axis=0, tiled=True)  29.5 us
  transfers between devices with their start and end apart: 9, of which 9 were waited for; matrix products, arithmetic and copies ran while one was open for 4% of the time, Pallas kernels for 0%

commit v1 on v0

v1 whole, which is shorter than its diff:
```python
import functools
import math

import jax
import jax.numpy as jnp
from jax import lax
from jax.experimental import pallas as pl
from jax.experimental.pallas import tpu as pltpu
from jax.sharding import PartitionSpec as P

HEADS = 12
HEAD = 64
A_DEV = 16
D = 768
ROWS = 512
WIDE = D + 128
CHUNKS = 4
UNIT = (48, 384)
F32 = jnp.float32
BF16 = jnp.bfloat16
MESH = pl.DeviceIdType.MESH


def place():
    dp, seq, xl = lax.axis_index("dp"), lax.axis_index("seq"), lax.axis_index("cell")
    return dp, seq // 2, seq % 2, xl


def remote(src, dst, send, recv, device):
    return pltpu.make_async_remote_copy(
        src_ref=src, dst_ref=dst, send_sem=send, recv_sem=recv, device_id=device, device_id_type=MESH
    )


def greet(peers):
    barrier = pltpu.get_barrier_semaphore()
    for peer in peers:
        pl.semaphore_signal(barrier, inc=1, device_id=peer, device_id_type=MESH)
    pl.semaphore_wait(barrier, len(peers))


def sample_peers(dp, z, c, xl):
    return [
        (dp, lax.rem(z + dz, 8) * 2 + c, lax.rem(xl + dx, 2))
        for dz in (4, 3, 5, 2, 6, 1, 7, 0)
        for dx in (1, 0)
        if (dz, dx) != (0, 0)
    ]


PEER_STEPS = [(dz, dx) for dz in (4, 3, 5, 2, 6, 1, 7, 0) for dx in (1, 0) if (dz, dx) != (0, 0)]


def pool_kernel(
    count_ref, ids_ref, cells_ref, gain_ref, out_ref,
    core_out, core_in, own, sent, got, every,
    core_send, core_recv, peer_send, peer_recv, spread_send, spread_recv, twin_send, twin_recv,
):
    dp, z, c, xl = place()
    twin = (dp, z * 2 + 1 - c, xl)
    peers = sample_peers(dp, z, c, xl)
    greet([twin] + peers)
    ids = ids_ref[...]
    valid = lax.broadcasted_iota(jnp.int32, (1, ROWS), 1) < count_ref[0, 0]
    ids = jnp.where(valid, ids, -1)
    row = lax.broadcasted_iota(jnp.int32, (256, ROWS), 0)
    base = (row // 32) * 64 + row % 32

    def partial_sums(core):
        hot = jnp.where(ids == base + core * 32, 1.0, 0.0).astype(BF16)
        sums = jnp.dot(hot, cells_ref[...], preferred_element_type=F32)
        counts = jnp.dot(hot, jnp.ones((ROWS, 128), BF16), preferred_element_type=F32)
        return sums, counts

    sums, counts = partial_sums(1 - c)
    core_out[:, :D] = sums.astype(BF16)
    core_out[:, D:] = counts.astype(BF16)
    first = remote(core_out, core_in, core_send, core_recv, twin)
    first.start()
    sums, counts = partial_sums(c)
    own[:, :D] = sums
    own[:, D:] = counts
    first.wait_recv()
    own[...] += core_in[...].astype(F32)
    sent[...] = own[...].astype(BF16).reshape(16, 16, WIDE)
    copies = []
    for at, ((dz, dx), peer) in enumerate(zip(PEER_STEPS, peers)):
        there = lax.rem(z + dz, 8) * 2 + lax.rem(xl + dx, 2)
        copy = remote(sent.at[there], got.at[at], peer_send.at[at], peer_recv.at[at], peer)
        copy.start()
        copies.append(copy)
    me = z * 2 + xl
    total = own[pl.ds(pl.multiple_of(me * 16, 16), 16), :]
    for at in reversed(range(15)):
        copies[at].wait_recv()
        total = total + got[at].astype(F32)
    pooled = total[:, :D] / jnp.maximum(total[:, D : D + 1], 1.0)
    scale = lax.rsqrt(jnp.mean(pooled * pooled, axis=1, keepdims=True) + 1e-06)
    every[c, me] = (pooled * scale * gain_ref[...]).astype(BF16)
    spreads = []
    for at, peer in enumerate(peers):
        copy = remote(every.at[c, me], every.at[c, me], spread_send.at[at], spread_recv.at[at], peer)
        copy.start()
        spreads.append(copy)
    twins = []
    for at in [15] + list(reversed(range(15))):
        if at == 15:
            here = me
        else:
            dz, dx = PEER_STEPS[at]
            here = lax.rem(z + 8 - dz, 8) * 2 + lax.rem(xl + dx, 2)
            remote(
                every.at[c, here], every.at[c, here], spread_send.at[at], spread_recv.at[at], peers[at]
            ).wait_recv()
        copy = remote(every.at[c, here], every.at[c, here], twin_send.at[at], twin_recv.at[at], twin)
        copy.start()
        twins.append(copy)
    for copy in twins:
        copy.wait_recv()
    out_ref[...] = every[...]
    first.wait_send()
    for copy in copies + spreads + twins:
        copy.wait_send()


def pool(count, ids, cells, gain):
    vmem = pl.BlockSpec(memory_space=pltpu.VMEM)
    dma = pltpu.SemaphoreType.DMA
    return pl.pallas_call(
        pool_kernel,
        out_shape=jax.ShapeDtypeStruct((2, 16, A_DEV, D), BF16),
        in_specs=[pl.BlockSpec(memory_space=pltpu.SMEM), vmem, vmem, vmem],
        out_specs=vmem,
        scratch_shapes=[
            pltpu.VMEM((256, WIDE), BF16),
            pltpu.VMEM((256, WIDE), BF16),
            pltpu.VMEM((256, WIDE), F32),
            pltpu.VMEM((16, 16, WIDE), BF16),
            pltpu.VMEM((15, 16, WIDE), BF16),
            pltpu.VMEM((2, 16, A_DEV, D), BF16),
            dma, dma, dma((15,)), dma((15,)), dma((15,)), dma((15,)), dma((16,)), dma((16,)),
        ],
        compiler_params=pltpu.CompilerParams(
            collective_id=0, has_side_effects=True, vmem_limit_bytes=32 * 1024 * 1024
        ),
        cost_estimate=pl.CostEstimate(flops=10**9, bytes_accessed=4 * 10**6, transcendentals=0),
    )(count, ids, cells, gain)


def reduce_kernel(
    g_ref, out_ref, twin_in, first_out, first_in, second_out, second_in, root_out, root_in, last,
    twin_send, twin_recv, first_send, first_recv, second_send, second_recv,
    root_send, root_recv, last_send, last_recv,
):
    dp, z, c, xl = place()
    y, xh = dp // 2, dp % 2
    x = xh * 2 + xl
    seq = z * 2 + c
    twin = (dp, z * 2 + 1 - c, xl)
    my_first = jnp.where(c == 0, x, y)
    my_second = jnp.where(c == 0, y, x)

    def along_x(to):
        return (y * 2 + to // 2, seq, lax.rem(to, 2))

    def along_y(to):
        return (to * 2 + xh, seq, xl)

    def choose(to, is_x):
        a, b = along_x(to), along_y(to)
        return tuple(jnp.where(is_x, i, j) for i, j in zip(a, b))

    def step(at, j):
        return lax.rem(at + j, 4)

    firsts = [choose(step(my_first, j), c == 0) for j in (1, 2, 3)]
    seconds = [choose(step(my_second, j), c == 1) for j in (1, 2, 3)]
    others = [(lax.rem(dp + j, 8), seq, xl) for j in range(1, 8)]
    greet(
        [twin]
        + [along_x(step(x, j)) for j in (1, 2, 3)]
        + [along_y(step(y, j)) for j in (1, 2, 3)]
        + [(step(y, j) * 2 + 1 - xh, seq, xl) for j in (1, 2, 3)]
        + [(dp, lax.rem(z + j, 8) * 2 + c, xl) for j in range(1, 8)]
    )
    sends = []

    def twin_copy(k):
        return remote(g_ref.at[k, 1 - c], twin_in.at[k], twin_send.at[k], twin_recv.at[k], twin)

    def first_copy(k, j):
        to = step(my_first, j)
        return remote(
            first_out.at[k, to], first_in.at[k, j - 1], first_send.at[k, j - 1], first_recv.at[k, j - 1],
            firsts[j - 1],
        )

    def second_copy(k, j):
        to = step(my_second, j)
        return remote(
            second_out.at[k, to], second_in.at[k, j - 1], second_send.at[k, j - 1],
            second_recv.at[k, j - 1], seconds[j - 1],
        )

    root = (dp, dp * 2 + c, xl)
    is_root = z == dp

    def last_copy(k, j):
        return remote(last.at[k], last.at[k], last_send.at[k, j - 1], last_recv.at[k], others[j - 1])

    def stage0(k):
        twin_copy(k).start()

    def stage1(k):
        twin_copy(k).wait_recv()

        def unit(u, _):
            to = jnp.where(c == 0, (u % 4) * 4 + u // 4, u)
            both = g_ref[k, c, u].astype(F32) + twin_in[k, u].astype(F32)
            first_out[k, to // 4, to % 4] = both.astype(BF16)
            return 0

        lax.fori_loop(0, 16, unit, 0)
        for j in (2, 1, 3):
            first_copy(k, j).start()

    def stage2(k):
        for j in (1, 3, 2):
            first_copy(k, j).wait_recv()

        def unit(b, _):
            total = first_out[k, my_first, b].astype(F32)
            for j in range(3):
                total = total + first_in[k, j, b].astype(F32)
            second_out[k, b] = total.astype(BF16)
            return 0

        lax.fori_loop(0, 4, unit, 0)
        for j in (2, 1, 3):
            second_copy(k, j).start()

    def stage3(k):
        for j in (1, 3, 2):
            second_copy(k, j).wait_recv()
        total = second_out[k, my_second].astype(F32)
        for j in range(3):
            total = total + second_in[k, j].astype(F32)
        root_out[k] = total.astype(BF16)

        @pl.when(jnp.logical_not(is_root))
        def _():
            at = lax.rem(z - dp + 8, 8) - 1
            remote(root_out.at[k], root_in.at[k, at], root_send.at[k], root_recv.at[k, at], root).start()

    def stage4(k):
        @pl.when(is_root)
        def _():
            total = root_out[k].astype(F32)
            for j in range(7):
                remote(root_out.at[k], root_in.at[k, j], root_send.at[k], root_recv.at[k, j], twin).wait_recv()
                total = total + root_in[k, j].astype(F32)
            last[k] = total.astype(BF16)
            for j in range(1, 8):
                last_copy(k, j).start()

    def stage5(k):
        @pl.when(jnp.logical_not(is_root))
        def _():
            last_copy(k, 1).wait_recv()

        out_ref[k] = last[k].astype(F32)

    stages = [stage0, stage1, stage2, stage3, stage4, stage5]
    for tick in range(CHUNKS + len(stages) - 1):
        for s in reversed(range(len(stages))):
            if 0 <= tick - s < CHUNKS:
                stages[s](tick - s)

    for k in range(CHUNKS):
        twin_copy(k).wait_send()
        for j in (1, 2, 3):
            first_copy(k, j).wait_send()
            second_copy(k, j).wait_send()

        @pl.when(jnp.logical_not(is_root))
        def _():
            remote(root_out.at[k], root_in.at[k, 0], root_send.at[k], root_recv.at[k, 0], root).wait_send()

        @pl.when(is_root)
        def _():
            for j in range(1, 8):
                last_copy(k, j).wait_send()


def reduce_all(grads):
    vmem = pl.BlockSpec(memory_space=pltpu.VMEM)
    dma = pltpu.SemaphoreType.DMA
    return pl.pallas_call(
        reduce_kernel,
        out_shape=jax.ShapeDtypeStruct((CHUNKS, *UNIT), F32),
        in_specs=[vmem],
        out_specs=vmem,
        scratch_shapes=[
            pltpu.VMEM((CHUNKS, 16, *UNIT), BF16),
            pltpu.VMEM((CHUNKS, 4, 4, *UNIT), BF16),
            pltpu.VMEM((CHUNKS, 3, 4, *UNIT), BF16),
            pltpu.VMEM((CHUNKS, 4, *UNIT), BF16),
            pltpu.VMEM((CHUNKS, 3, *UNIT), BF16),
            pltpu.VMEM((CHUNKS, *UNIT), BF16),
            pltpu.VMEM((CHUNKS, 7, *UNIT), BF16),
            pltpu.VMEM((CHUNKS, *UNIT), BF16),
            dma((CHUNKS,)), dma((CHUNKS,)),
            dma((CHUNKS, 3)), dma((CHUNKS, 3)),
            dma((CHUNKS, 3)), dma((CHUNKS, 3)),
            dma((CHUNKS,)), dma((CHUNKS, 7)),
            dma((CHUNKS, 7)), dma((CHUNKS,)),
        ],
        compiler_params=pltpu.CompilerParams(
            collective_id=1, has_side_effects=True, vmem_limit_bytes=40 * 1024 * 1024
        ),
        cost_estimate=pl.CostEstimate(flops=10**7, bytes_accessed=5 * 10**6, transcendentals=0),
    )(grads)


def split_heads(matrix):
    return matrix.reshape(matrix.shape[0], HEADS, matrix.shape[1] // HEADS)


def shards(cells, anchor_ids, cell_counts, anchor_gain, w_query, w_keyval, w_out, cotangent):
    cell_rows = cells[0]
    n_rows = ROWS
    score_scale = 1.0 / math.sqrt(HEAD)
    valid_mask = jnp.arange(n_rows, dtype=jnp.int32) < cell_counts[0, 0]
    is_valid = valid_mask.astype(F32)
    normed = pool(cell_counts, anchor_ids, cell_rows, anchor_gain[None, :]).reshape(512, D)
    keyval = jnp.dot(normed, w_keyval, preferred_element_type=F32).astype(BF16)
    queries = jnp.dot(cell_rows, w_query, preferred_element_type=F32).astype(BF16)
    query_heads = split_heads(queries)
    key_heads = split_heads(keyval[:, :D])
    value_heads = split_heads(keyval[:, D:])
    logits = (
        jnp.einsum("chd,ahd->hca", query_heads, key_heads, preferred_element_type=F32) * score_scale
    )
    row_peak = jnp.max(logits, axis=2)
    exp_terms = jnp.exp(logits - row_peak[:, :, None])
    weighted = jnp.einsum(
        "hca,ahd->hcd", exp_terms.astype(BF16), value_heads, preferred_element_type=F32
    )
    row_total = jnp.sum(exp_terms, axis=2)
    attended = (
        jnp.transpose(weighted / row_total[:, :, None], (1, 0, 2)).reshape(n_rows, D).astype(BF16)
    )
    cell_delta = jnp.dot(attended, w_out, preferred_element_type=F32) * is_valid[:, None]
    cell_update = cell_delta.astype(BF16)[None]
    masked = cotangent[0] * valid_mask[:, None].astype(BF16)
    grad_out = jnp.einsum("cd,ce->de", attended, masked, preferred_element_type=F32)
    d_attended = jnp.einsum("ce,de->cd", masked, w_out, preferred_element_type=F32).astype(BF16)
    d_heads = split_heads(d_attended)
    row_delta = jnp.transpose(
        jnp.sum(d_heads.astype(F32) * split_heads(attended).astype(F32), axis=2)
    )
    attn_prob = exp_terms / row_total[:, :, None]
    d_prob = jnp.einsum("chd,ahd->hca", d_heads, value_heads, preferred_element_type=F32)
    d_logits = (attn_prob * (d_prob - row_delta[:, :, None]) * score_scale).astype(BF16)
    d_query = jnp.einsum("hca,ahd->chd", d_logits, key_heads, preferred_element_type=F32)
    d_key = jnp.einsum("hca,chd->ahd", d_logits, query_heads, preferred_element_type=F32)
    d_value = jnp.einsum(
        "hca,chd->ahd", attn_prob.astype(BF16), d_heads, preferred_element_type=F32
    )
    d_query = d_query.reshape(n_rows, D).astype(BF16)
    grad_query = jnp.einsum("cd,ce->de", cell_rows, d_query, preferred_element_type=F32)
    d_keyval = jnp.concatenate([d_key.reshape(512, D), d_value.reshape(512, D)], axis=1)
    grad_keyval = jnp.einsum("ad,ae->de", normed, d_keyval.astype(BF16), preferred_element_type=F32)
    chunks = [grad_out]
    for quad in range(3):
        cols = slice(quad * 256, quad * 256 + 256)
        vals = slice(D + quad * 256, D + quad * 256 + 256)
        chunks.append(
            jnp.concatenate([grad_query[:, cols], grad_keyval[:, cols], grad_keyval[:, vals]], axis=1)
        )
    grads = jnp.stack(chunks).astype(BF16).reshape(CHUNKS, 8, 2, 2, 24, 2, 384)
    grads = jnp.transpose(grads, (0, 2, 1, 3, 5, 4, 6)).reshape(CHUNKS, 2, 16, *UNIT)
    done = reduce_all(grads)
    done = jnp.concatenate([done[:, :24], done[:, 24:]], axis=2)
    return (
        cell_update,
        jnp.concatenate([done[1 + q, :, :256] for q in range(3)], axis=1),
        jnp.concatenate(
            [done[1 + q, :, 256:512] for q in range(3)] + [done[1 + q, :, 512:] for q in range(3)], axis=1
        ),
        done[0],
    )


def solution(mesh):
    return jax.shard_map(
        shards,
        mesh=mesh,
        in_specs=(
            P("dp", ("seq", "cell"), None),
            P("dp", ("seq", "cell")),
            P("dp", ("seq", "cell")),
            P(),
            P(),
            P(),
            P(),
            P("dp", ("seq", "cell"), None),
        ),
        out_specs=(
            P("dp", ("seq", "cell"), None),
            P(("seq", "cell"), None),
            P(("seq", "cell"), None),
            P(("seq", "cell"), None),
        ),
        check_vma=False,
    )
```

time: 818 us -> 159 us (0.19)
  waiting for transfers between devices: 701 us -> 0 us
  Pallas kernels: 0 us -> 86.5 us
  starting transfers between devices: 15.9 us -> 0 us
  between operations: 15.1 us -> 1.78 us
  matrix products: 45.5 us -> 33.9 us
    reduce_scatter x2 -> x0, waiting for transfers between devices: 238 us -> none  [the longest x1 121 us: shards(): lax.psum_scatter(grad_keyval_part.astype(jnp.bfloat16), ('seq', 'cell'),...]
    unnamed x9 -> x0, waiting for transfers between devices: 217 us -> none
    psum x2 -> x0, waiting for transfers between devices: 174 us -> none  [the longest x1 91.8 us: shards(): lax.psum(shares[0].astype(jnp.bfloat16), 'dp').astype(jnp.float32)]
    pallas_call x0 -> x2, Pallas kernels: none -> 86.5 us  [the longest x1 52.5 us: reduce_all(): pl.pallas_call(reduce_kernel, out_shape=jax.ShapeDtypeStruct((CHUNKS, *UN...]
    all_to_all x2 -> x0, waiting for transfers between devices: 41.6 us -> none  [the longest x1 37.9 us: shards(): lax.all_to_all(send_rows.reshape(owners, capacity, model_width), ('seq',...]
    all_gather x1 -> x0, waiting for transfers between devices: 29.5 us -> none  [shards(): key_piece = lax.all_gather(pair_block, 'seq', axis=0, tiled=True)]
    all_to_all x2 -> x0, starting transfers between devices: 15.4 us -> none  [the longest x1 9.65 us: shards(): lax.all_to_all(send_ids.reshape(owners, capacity), ('seq', 'cell'), split...]
    dot_general x15 -> x12, matrix products: 43.5 us -> 31.9 us  [the longest x1 8.52 us: shards(): jnp.einsum('hca,ahd->hcd', exp_terms.astype(BF16), value_heads, preferred...]
  transfers between devices with their start and end apart: 9 -> 0, of which waited for: 9 -> 0; matrix products, arithmetic and copies ran while one was open for 4% -> 0% of each run, Pallas kernels for 0% -> 0%
where the time goes in v1:
time: 159 us; the launch traced here: 158 us
  Pallas kernels  86.5 us (54%)
  matrix products  33.9 us (21%)
  local copies, waits for them, and re-layouts  30.4 us (19%)
  other arithmetic  5.63 us (4%)
  between operations  1.78 us (1%)
    pallas_call x1, Pallas kernels, reduce_all(): pl.pallas_call(reduce_kernel, out_shape=jax.ShapeDtypeStruct((CHUNKS, *UN...  52.5 us
    pallas_call x1, Pallas kernels, pool(): pl.pallas_call(pool_kernel, out_shape=jax.ShapeDtypeStruct((2, 16, A_DEV,...  34 us
    dot_general x1, matrix products, shards(): jnp.einsum('hca,ahd->hcd', exp_terms.astype(BF16), value_heads, preferred...  8.52 us
    another operation x6, local copies, waits for them, and re-layouts, shards(): grads = jnp.stack(chunks).astype(BF16).reshape(CHUNKS, 8, 2, 2, 24, 2, 384)  8.29 us
    unnamed x42, local copies, waits for them, and re-layouts  6.2 us
    dot_general x1, matrix products, shards(): jnp.einsum('chd,ahd->hca', d_heads, value_heads, preferred_element_type=F32)  4.22 us

profile of v1, /device:TPU:32, one launch (start us, length us, event | category | flops | bytes accessed | tf_op | source)
XLA Modules:
  0.0 158.2 jit_solution(13078178864566831366)
XLA Ops:
  0.6 0.0 copy-start
  1.4 0.7 broadcast_in_dim.4.gain_ref
  2.1 1.1 copy-done.2
  3.3 0.7 copy-done.4
  4.0 34.0 %shard_map.111 = bf16[2,16,16,768]{3,2,1,0:T(8,128)(2,1)S(1)} custom-call(s32[1,1]{1,0:T(1,128)} %copy.59.count_ref, s32[1,512]{1,0:T(1,128)S(1)} %copy-done.4, bf16[512,768]{1,0:T(8,128)(2,1)S(1)} %bitcast.104, f32[1,768]{1,0:T(1,128)S(1)} %broadcast_in_dim.4.gain_ref), custom_call_target="tpu_custom_call" | custom-call | flops 1000000000 | bytes 4000000 | tf_op jit(solution)/shard_map/pallas_call | solution.py:129
  38.0 0.0 copy-done
  38.0 1.4 convolution_convert_fusion.1
  39.4 0.0 copy-start.3
  39.4 1.1 fusion.35
  40.5 0.3 copy.28
  40.8 0.0 copy-done.3
  40.8 2.9 %convolution_convert_fusion.5 = bf16[512,768]{1,0:T(8,128)(2,1)} fusion(bf16[768,768]{1,0:T(8,128)(2,1)} %param.12, bf16[1,512,768]{2,1,0:T(8,128)(2,1)S(1)} %copy-done.3), kind=kOutput, calls=%fused_computation.26 | convolution fusion | flops 604372992 | bytes 2752512 | tf_op jit(solution)/shard_map/dot_general | solution.py:337
  43.7 1.4 copy.27
  45.1 1.8 %multiply_reduce_fusion = (f32[12,512]{1,0:T(8,128)S(1)}, f32[12,512,512]{1,2,0:T(8,128)S(1)}) fusion(bf16[512,12,64]{0,2,1:T(8,128)(2,1)S(1)} %bitcast.109, bf16[512,12,64]{0,2,1:T(8,128)(2,1)S(1)} %bitcast.107), kind=kOutput, calls=%fused_computation.2 | convolution fusion | flops 408938496 | bytes 14180352 | tf_op jit(solution)/shard_map/chd,ahd->hca/dot_general | solution.py:342
  47.0 0.0 copy-start.5
  47.0 0.0 copy-start.15
  47.0 2.1 %fusion.1 = f32[12,512]{1,0:T(8,128)S(1)} fusion(f32[12,512,512]{1,2,0:T(8,128)S(1)} %get-tuple-element.21, f32[12,512]{1,0:T(8,128)S(1)} %get-tuple-element.20), kind=kLoop, calls=%fused_computation.4 | loop fusion | flops 9431040 | bytes 12632064 | tf_op jit(solution)/shard_map/reduce_sum | solution.py:349
  49.1 2.4 %copy-done.5 = f32[12,512,512]{1,2,0:T(8,128)} copy-done((f32[12,512,512]{1,2,0:T(8,128)}, f32[12,512,512]{1,2,0:T(8,128)S(1)}, u32[]{:S(2)}) %copy-start.5) | copy-done | bytes 12582936
  51.5 0.0 copy-done.15
  51.5 3.0 %convolution_convert_fusion.4 = bf16[512,768]{1,0:T(8,128)(2,1)} fusion(bf16[768,768]{1,0:T(8,128)(2,1)} %param.14, bf16[1,512,768]{2,1,0:T(8,128)(2,1)S(1)} %copy-done.15, bf16[512]{0:T(512)(128)(2,1)S(1)} %get-tuple-element.24), kind=kOutput, calls=%fused_computation.25 | convolution fusion | flops 604766208 | bytes 2753536 | tf_op jit(solution)/shard_map/ce,de->cd/dot_general | solution.py:357
  54.5 2.3 %copy.32 = bf16[512,768]{0,1:T(8,128)(2,1)} copy(bf16[512,768]{1,0:T(8,128)(2,1)} %convolution_convert_fusion.4) | data formatting | bytes 1572864 | tf_op jit(solution)/shard_map/convert_element_type | solution.py:357
  56.8 2.3 %copy.29 = bf16[512,768]{0,1:T(8,128)(2,1)} copy(bf16[512,768]{1,0:T(8,128)(2,1)} %get-tuple-element.11) | data formatting | bytes 1572864 | tf_op jit(solution)/shard_map/slice | solution.py:340
  59.1 8.5 %multiply_reduce_fusion.1 = (f32[512,12]{0,1:T(8,128)S(1)}, bf16[512,12,64]{0,2,1:T(8,128)(2,1)}) fusion(bf16[512,12,64]{0,2,1:T(8,128)(2,1)} %bitcast.112, f32[512,12]{0,1:T(8,128)S(1)} %bitcast.119, bf16[512,12,64]{0,2,1:T(8,128)(2,1)} %bitcast.115, f32[12,512,512]{1,2,0:T(8,128)} %copy-done.5, f32[12,512]{1,0:T(8,128)S(1)} %get-tuple-element.20), kind=kOutput, calls=%fused_computation.19 | convolution fusion | flops 414443520 | bytes 15015936 | tf_op jit(solution)/shard_map/hca,ahd->hcd/dot_general | solution.py:346
  67.6 0.1 copy-done.6
  67.8 0.4 copy-done.13
  68.1 0.2 copy-done.14
  68.4 4.2 %multiply_convert_fusion = bf16[12,512,512]{1,2,0:T(8,128)(2,1)S(1)} fusion(f32[12,512]{1,0:T(8,128)S(1)} %bitcast.123, bf16[512,12,64]{0,2,1:T(8,128)(2,1)S(1)} %bitcast.113, bf16[512,12,64]{0,2,1:T(8,128)(2,1)S(1)} %bitcast.116, f32[12,512]{1,0:T(8,128)S(1)} %fusion.1, f32[12,512]{1,0:T(8,128)S(1)} %get-tuple-element.20, f32[12,512,512]{1,2,0:T(8,128)S(1)} %copy-done.6), kind=kOutput, calls=%fused_computation | convolution fusion | flops 424673280 | bytes 20520960 | tf_op jit(solution)/shard_map/chd,ahd->hca/dot_general | solution.py:363
  72.6 1.1 convolution_convert_fusion.7
  73.7 0.8 fusion.17
  74.5 1.0 fusion.36
  75.5 2.0 %convolution_convert_fusion.6 = bf16[12,64,512]{2,1,0:T(8,128)(2,1)S(1)} fusion(bf16[512,12,64]{0,2,1:T(8,128)(2,1)S(1)} %bitcast.110, bf16[12,512,512]{1,2,0:T(8,128)(2,1)S(1)} %multiply_convert_fusion), kind=kOutput, calls=%fused_computation.27 | convolution fusion | flops 403046400 | bytes 7864320 | tf_op jit(solution)/shard_map/hca,chd->ahd/dot_general | solution.py:366
  77.5 2.8 %fusion.18 = bf16[12,64,512]{2,1,0:T(8,128)(2,1)S(1)} fusion(bf16[512,12,64]{0,2,1:T(8,128)(2,1)S(1)} %bitcast.114, f32[12,512]{1,0:T(8,128)S(1)} %fusion.1, f32[12,512]{1,0:T(8,128)S(1)} %get-tuple-element.20, f32[12,512,512]{1,2,0:T(8,128)S(1)} %copy-done.6), kind=kOutput, calls=%fused_computation.29 | convolution fusion | flops 415629312 | bytes 14204928 | tf_op jit(solution)/shard_map/hca,chd->ahd/dot_general | solution.py:367
  80.3 1.4 convolution_convert_fusion
  81.7 1.2 fusion.34
  82.9 0.1 pad_maximum_fusion
  83.0 0.6 copy.38
  83.6 0.3 stack.13
  84.0 0.2 copy.41
  84.1 0.8 copy-done.8
  84.9 0.1 copy-done.11
  85.0 0.1 copy-done.12
  85.2 0.1 pad_maximum_fusion.1
  85.2 0.6 copy.39
  85.9 1.2 stack.14
  87.1 1.5 copy.42
  88.7 0.0 copy-done.10
  88.7 0.1 pad_maximum_fusion.2
  88.8 1.5 copy.40
  90.2 3.5 %stack.15 = bf16[1,8,2,2,24,2,384]{6,5,4,3,2,1,0:T(2,128)(2,1)} reshape(bf16[768,768]{1,0:T(8,128)(2,1)} %copy.40) | data formatting | bytes 2359296 | tf_op jit(solution)/shard_map/stack | solution.py:381
  93.8 1.5 copy.43
  95.3 1.0 multiply_bitcast_fusion
  96.3 2.3 %copy.53 = bf16[768,512]{1,0:T(8,128)(2,1)} copy(bf16[768,512]{0,1:T(8,128)(2,1)} %multiply_bitcast_fusion) | data formatting | bytes 1572864 | tf_op jit(solution)/shard_map/cd,ce->de/dot_general | solution.py:356
  98.6 2.2 %fusion.16 = bf16[1,8,2,2,24,2,384]{6,4,5,3,2,1,0:T(8,128)(2,1)S(1)} fusion(bf16[8,2,2,24,512,1]{4,3,5,2,1,0:T(8,128)(2,1)} %bitcast.120, bf16[2,384,512,1,1,1]{2,1,0,5,4,3:T(8,128)(2,1)} %bitcast.117), kind=kOutput, calls=%fused_computation.23 | convolution fusion | flops 604569600 | bytes 2752512 | tf_op jit(solution)/shard_map/cd,ce->de/dot_general | solution.py:356
  100.8 1.0 maximum_bitcast_fusion
  101.8 0.6 copy.44
  102.5 52.5 %shard_map.112 = f32[4,48,384]{2,1,0:T(8,128)S(1)} custom-call(bf16[4,2,16,48,384]{4,3,2,1,0:T(8,128)(2,1)S(1)} %bitcast.103), custom_call_target="tpu_custom_call" | custom-call | flops 10000000 | bytes 5000000 | tf_op jit(solution)/shard_map/pallas_call | solution.py:298
  155.0 0.0 copy-start.18
  155.0 0.0 copy-start.19
  155.0 0.6 fusion.23
  155.7 0.0 copy-start.17
  155.8 0.6 pad_maximum_fusion.4
  156.4 0.0 copy-done.18
  156.4 0.1 copy-done.19
  156.5 1.7 %fusion.21 = bf16[1,512,768]{2,1,0:T(8,128)(2,1)} fusion(bf16[512,768]{0,1:T(8,128)(2,1)S(1)} %bitcast.121, bf16[768,768]{1,0:T(8,128)(2,1)S(1)} %copy-done.18, f32[512]{0:T(512)S(1)} %get-tuple-element.25), kind=kOutput, calls=%fused_computation.30 | convolution fusion | flops 604766208 | bytes 2754560 | tf_op jit(solution)/shard_map/dot_general | solution.py:353
  (27 shorter events, 0.1 us)
Async XLA Ops:
  0.6 37.4 %copy-start = (bf16[768,1536]{1,0:T(8,128)(2,1)S(1)}, bf16[768,1536]{1,0:T(8,128)(2,1)}, u32[]{:S(2)}) copy-start(bf16[768,1536]{1,0:T(8,128)(2,1)} %param.13) | copy-start | bytes 7077892
  2.1 1.1 copy-start.2
  3.3 0.7 copy-start.4
  39.4 1.4 copy-start.3
  47.0 4.5 %copy-start.5 = (f32[12,512,512]{1,2,0:T(8,128)}, f32[12,512,512]{1,2,0:T(8,128)S(1)}, u32[]{:S(2)}) copy-start(f32[12,512,512]{1,2,0:T(8,128)S(1)} %get-tuple-element.21) | copy-start | bytes 37748740
  47.0 4.5 %copy-start.15 = (bf16[1,512,768]{2,1,0:T(8,128)(2,1)S(1)}, bf16[1,512,768]{2,1,0:T(8,128)(2,1)}, u32[]{:S(2)}) copy-start(bf16[1,512,768]{2,1,0:T(8,128)(2,1)} %param.15) | copy-start | bytes 2359300
  59.1 8.7 %copy-start.6 = (f32[12,512,512]{1,2,0:T(8,128)S(1)}, f32[12,512,512]{1,2,0:T(8,128)}, u32[]{:S(2)}) copy-start(f32[12,512,512]{1,2,0:T(8,128)} %copy-done.5) | copy-start | bytes 37748740
  59.1 9.0 %copy-start.13 = (bf16[512,768]{0,1:T(8,128)(2,1)S(1)}, bf16[512,768]{0,1:T(8,128)(2,1)}, u32[]{:S(2)}) copy-start(bf16[512,768]{0,1:T(8,128)(2,1)} %copy.32) | copy-start | bytes 2359300
  59.1 9.2 %copy-start.14 = (bf16[512,768]{0,1:T(8,128)(2,1)S(1)}, bf16[512,768]{0,1:T(8,128)(2,1)}, u32[]{:S(2)}) copy-start(bf16[512,768]{0,1:T(8,128)(2,1)} %copy.29) | copy-start | bytes 2359300
  83.9 1.0 copy-start.8
  83.9 1.1 copy-start.11
  83.9 1.2 copy-start.12
  87.1 1.6 copy-start.7
  87.1 1.6 copy-start.9
  87.1 1.6 %copy-start.10 = (bf16[768,256]{0,1:T(8,128)(2,1)S(1)}, bf16[768,256]{0,1:T(8,128)(2,1)}, u32[]{:S(2)}) copy-start(bf16[768,256]{0,1:T(8,128)(2,1)} %get-tuple-element.6) | copy-start | bytes 1179652
  93.8 1.5 copy-start.16
  155.0 1.4 copy-start.18
  155.0 1.5 copy-start.19
  155.7 2.5 %copy-start.1 = (bf16[768,1536]{1,0:T(8,128)(2,1)S(1)}, bf16[768,1536]{1,0:T(8,128)(2,1)}, u32[]{:S(2)}) copy-start(bf16[768,1536]{1,0:T(8,128)(2,1)} %param.13) | copy-start | bytes 7077892
  155.7 2.5 %copy-start.17 = (f32[24,1536]{1,0:T(8,128)}, f32[24,1536]{1,0:T(8,128)S(1)}, u32[]{:S(2)}) copy-start(f32[24,1536]{1,0:T(8,128)S(1)} %bitcast_dynamic-update-slice_fusion) | copy-start | bytes 442372
